TPU v7x, 256 devices: a whole 4x4x8 slice. The times are simulated.
256 devices in a mesh: seq: 64 (over z_lo, y, x, core), mp: 4 (over z_hi).
Axes of the slice: x: 4, y: 4, z: 8 (z_hi: 4, z_lo: 2; z = z_hi * 2 + z_lo), core: 2. Of those that a mesh axis runs over, the one named last changes fastest.
Arguments:
- byte_states: bfloat16 [32768, 1024], P('seq'), may hold values from -6 to 6
- byte_patch: int32 [64, 512], P('seq'), may hold values from 0 to 15, as said below
- pool_score: bfloat16 [1024, 16], P(None, 'mp'), may hold values from -1 to 1
- w_query: bfloat16 [1024, 2048], P(None, 'mp'), may hold values from -1 to 1
- w_key: bfloat16 [1024, 2048], P(None, 'mp'), may hold values from -1 to 1
- w_value: bfloat16 [1024, 2048], P(None, 'mp'), may hold values from -0.1875 to 0.1875
- out_grad: bfloat16 [1024, 2048], P('seq', 'mp'), may hold values from -6 to 6
Outputs:
- grad_bytes: bfloat16 [32768, 1024], P('seq')
- grad_query: float32 [1024, 2048], P('seq', 'mp')
- grad_key: float32 [1024, 2048], P('seq', 'mp')
- grad_value: float32 [1024, 2048], P('seq', 'mp')
- grad_score: float32 [1024, 16], P('seq', 'mp')
Inputs may be any that keep to these rules, and one draw needn't show every extreme that they name: `byte_patch`: in each row the patch index starts at 0, never falls and rises by at most 1 from byte to byte; in some row it reaches 15.
All inputs are finite; a program needn't handle non-finite values.
Results may differ from a plain program's by a relative error of at most 0.03.
The roundings to bfloat16 on the way count: a program that leaves them out, or rounds other values in their place, can miss the bound.
Values may be sent and summed in bfloat16 or wider, within the bound.
A program may use at most 64 MiB of HBM per device.

v0:
```python
import jax
import jax.numpy as jnp
from jax import lax
from jax.sharding import PartitionSpec as P

HD = 128
PMAX = 16


def segment_softmax(scores, member):
    peak = jnp.max(jnp.where(member[:, :, None], scores[None, :, :], -1e30), axis=1)
    byte_peak = jnp.sum(jnp.where(member[:, :, None], peak[:, None, :], 0.0), axis=0)
    expd = jnp.exp(scores - byte_peak)
    total = jnp.sum(jnp.where(member[:, :, None], expd[None, :, :], 0.0), axis=1)
    byte_total = jnp.sum(jnp.where(member[:, :, None], total[:, None, :], 0.0), axis=0)
    return expd / byte_total


def patch_sum_back(values, member):
    total = jnp.sum(jnp.where(member[:, :, None], values[None, :, :], 0.0), axis=1)
    return jnp.sum(jnp.where(member[:, :, None], total[:, None, :], 0.0), axis=0)


def shards(byte_states, byte_patch, pool_score, w_query, w_key, w_value, out_grad):
    ids = byte_patch[0]
    heads = pool_score.shape[1]
    width = w_query.shape[1]
    scale = HD ** (-0.5)
    member = ids[None, :] == jnp.arange(PMAX, dtype=jnp.int32)[:, None]
    onehot = member.astype(jnp.float32)
    count = ids[-1] + 1
    slot_valid = jnp.arange(PMAX, dtype=jnp.int32) < count
    scores = jnp.dot(byte_states, pool_score, preferred_element_type=jnp.float32)
    attn = segment_softmax(scores, member)
    spread = jnp.repeat(attn, HD, axis=1)
    weights = (w_query, w_key, w_value)
    projs = [jnp.dot(byte_states, weight, preferred_element_type=jnp.float32) for weight in weights]
    pooled = [
        jnp.dot(onehot, proj * spread, precision=lax.Precision.HIGHEST).astype(jnp.bfloat16)
        for proj in projs
    ]
    q_loc, k_loc, v_loc = pooled
    keys_all, values_all, valid_all = (
        lax.all_gather(k_loc, "seq", axis=0, tiled=True),
        lax.all_gather(v_loc, "seq", axis=0, tiled=True),
        lax.all_gather(slot_valid.astype(jnp.bfloat16), "seq", axis=0, tiled=True),
    )
    slots = keys_all.shape[0]
    me = lax.axis_index("seq")
    qpos = me * PMAX + jnp.arange(PMAX, dtype=jnp.int32)
    kpos = jnp.arange(slots, dtype=jnp.int32)
    mask = (kpos[None, :] <= qpos[:, None]) & (valid_all[None, :] > 0)
    qh = q_loc.reshape(PMAX, heads, HD)
    kh = keys_all.reshape(slots, heads, HD)
    vh = values_all.reshape(slots, heads, HD)
    g = jnp.where(slot_valid[:, None], out_grad, jnp.zeros_like(out_grad))
    gh = g.reshape(PMAX, heads, HD)
    s = jnp.einsum("qhd,khd->hqk", qh, kh, preferred_element_type=jnp.float32) * scale
    peak = jnp.max(jnp.where(mask[None], s, -1e30), axis=2, keepdims=True)
    expd = jnp.where(mask[None], jnp.exp(s - peak), 0.0)
    total = jnp.sum(expd, axis=2, keepdims=True)
    prob = expd / total
    pb = prob.astype(jnp.bfloat16)
    outv = jnp.einsum("hqk,khd->qhd", pb, vh, preferred_element_type=jnp.float32)
    delta = jnp.sum(gh.astype(jnp.float32) * outv, axis=2).T[:, :, None]
    dprob = jnp.einsum("qhd,khd->hqk", gh, vh, preferred_element_type=jnp.float32)
    dscore_att = (prob * (dprob - delta) * scale).astype(jnp.bfloat16)
    dq = (
        jnp.einsum("hqk,khd->qhd", dscore_att, kh, preferred_element_type=jnp.float32)
        .reshape(PMAX, width)
        .astype(jnp.bfloat16)
    )
    dk_part = jnp.einsum(
        "hqk,qhd->khd", dscore_att, qh, preferred_element_type=jnp.float32
    ).reshape(PMAX * lax.axis_size("seq"), width)
    dv_part = jnp.einsum("hqk,qhd->khd", pb, gh, preferred_element_type=jnp.float32).reshape(
        PMAX * lax.axis_size("seq"), width
    )
    summed = lax.psum_scatter(
        jnp.concatenate([dk_part, dv_part], axis=1), "seq", scatter_dimension=0, tiled=True
    )
    dk = summed[:, :width]
    dv = summed[:, width:]
    dk = dk.astype(jnp.bfloat16)
    dv = dv.astype(jnp.bfloat16)
    onehot_t = onehot.T
    dattn = jnp.zeros(projs[0].shape, jnp.float32)
    dys = []
    for proj, grad_p in zip(projs, (dq, dk, dv)):
        back_rows = jnp.dot(onehot_t, grad_p.astype(jnp.float32), precision=lax.Precision.HIGHEST)
        dys.append((spread * back_rows).astype(jnp.bfloat16))
        dattn = dattn + back_rows * proj
    dattn = jnp.sum(dattn.reshape(dattn.shape[0], heads, HD), axis=2)
    dscore = (attn * (dattn - patch_sum_back(attn * dattn, member))).astype(jnp.bfloat16)
    partial_grads = [
        lax.dot_general(
            byte_states, dy, (((0,), (0,)), ((), ())), preferred_element_type=jnp.float32
        )
        for dy in dys + [dscore]
    ]
    grad_query, grad_key, grad_value, grad_score = (
        lax.psum_scatter(partial_grads[0], "seq", scatter_dimension=0, tiled=True),
        lax.psum_scatter(partial_grads[1], "seq", scatter_dimension=0, tiled=True),
        lax.psum_scatter(partial_grads[2], "seq", scatter_dimension=0, tiled=True),
        lax.psum_scatter(partial_grads[3], "seq", scatter_dimension=0, tiled=True),
    )
    dx = jnp.dot(dys[0], w_query.T, preferred_element_type=jnp.float32)
    dx = dx + jnp.dot(dys[1], w_key.T, preferred_element_type=jnp.float32)
    dx = dx + jnp.dot(dys[2], w_value.T, preferred_element_type=jnp.float32)
    dx = dx + jnp.dot(dscore, pool_score.T, preferred_element_type=jnp.float32)
    grad_bytes = lax.psum(dx, "mp").astype(jnp.bfloat16)
    return (grad_bytes, grad_query, grad_key, grad_value, grad_score)


def solution(mesh):
    return jax.shard_map(
        shards,
        mesh=mesh,
        in_specs=(
            P("seq", None),
            P("seq", None),
            P(None, "mp"),
            P(None, "mp"),
            P(None, "mp"),
            P(None, "mp"),
            P("seq", "mp"),
        ),
        out_specs=(P("seq", None), P("seq", "mp"), P("seq", "mp"), P("seq", "mp"), P("seq", "mp")),
        check_vma=False,
    )
```

profile of v0, /device:TPU:1, one launch (start us, length us, event | category | flops | bytes accessed | tf_op | source)
XLA Modules:
  0.0 1698.6 jit_solution(4972429234983702938)
XLA Ops:
  9.8 2.0 fusion.81
  13.4 1.8 bitcast_multiply_fusion.3
  15.3 1.2 convolution_convert_fusion.3
  20.6 141.2 %all-reduce = bf16[1024]{0:T(1024)(128)(2,1)S(1)} all-reduce(bf16[1024]{0:T(1024)(128)(2,1)S(1)} %dynamic-update-slice), channel_id=1, replica_groups=mesh['seq'=64,'mp'=4] {'seq'}, use_global_device_ids=true, to_apply=%add | all-reduce | flops 1024 | bytes 4096
  162.5 1.6 convolution_multiply_fusion
  164.9 64.9 %all-gather.5.cloned.1.call-done = bf16[1024,512]{1,0:T(8,128)(2,1)} async-done(((bf16[16,512]{1,0:T(8,128)(2,1)}), bf16[1024,512]{1,0:T(8,128)(2,1)}) %all-gather.5.cloned.1.call-update) | async-done | bytes 1048592 | tf_op jit(solution)/shard_map/all_gather | solution.py:45
  229.9 1.6 fusion.14
  231.5 1.7 fusion.9
  233.7 2.5 pad_maximum_fusion
  236.2 5.3 copy.69
  243.4 284.3 %reduce-scatter.16.cloned.1.call-done = f32[16,1024]{1,0:T(8,128)} async-done(((f32[1024,1024]{1,0:T(8,128)}), f32[16,1024]{1,0:T(8,128)}) %reduce-scatter.16.cloned.1.call-update) | async-done | bytes 65552
  529.0 1.4 fusion.18
  533.7 1.8 convolution_bitcast_fusion.1
  535.5 1.8 copy.73
  537.4 1.8 convolution_bitcast_fusion
  539.2 1.9 copy.75
  541.3 1.8 convolution_bitcast_fusion.2
  543.0 1.9 copy.71
  550.4 66.6 %all-reduce.2 = bf16[512,1024]{1,0:T(8,128)(2,1)} all-reduce(f32[512,1024]{1,0:T(8,128)S(1)} %add_add_fusion), channel_id=1, replica_groups=mesh['seq'=64,'mp'=4] {'mp'}, use_global_device_ids=true, to_apply=%region_11.12 | all-reduce | flops 524288 | bytes 3145728 | tf_op jit(solution)/shard_map/psum | solution.py:111
  617.0 211.4 %reduce-scatter.24.cloned.1.call-done = f32[16,4]{1,0:T(8,128)} async-done(((f32[1024,4]{1,0:T(8,128)}), f32[16,4]{1,0:T(8,128)}) %reduce-scatter.24.cloned.1.call-update) | async-done | bytes 272
  828.4 1.3 copy.78
  829.7 286.3 %reduce-scatter.20.cloned.1.call-done = f32[16,512]{1,0:T(8,128)} async-done(((f32[1024,512]{1,0:T(8,128)}), f32[16,512]{1,0:T(8,128)}) %reduce-scatter.20.cloned.1.call-update) | async-done | bytes 32784
  1116.0 287.8 %reduce-scatter.22.cloned.1.call-done = f32[16,512]{1,0:T(8,128)} async-done(((f32[1024,512]{1,0:T(8,128)}), f32[16,512]{1,0:T(8,128)}) %reduce-scatter.22.cloned.1.call-update) | async-done | bytes 32784
  1403.9 287.9 %reduce-scatter.18.cloned.1.call-done = f32[16,512]{1,0:T(8,128)} async-done(((f32[1024,512]{1,0:T(8,128)}), f32[16,512]{1,0:T(8,128)}) %reduce-scatter.18.cloned.1.call-update) | async-done | bytes 32784
  (98 shorter events, 20.9 us)
Async XLA Ops:
  7.2 155.4 %all-gather.3.cloned.1.call-start = ((), (), s32[]{:S(2)}) async-start(), calls=%async_computation.5 | async-start | bytes 1064960 | tf_op jit(solution)/shard_map/all_gather | solution.py:44
  8.4 1.3 copy-start.20
  9.5 2.3 copy-start.12
  11.8 3.4 copy-start.6
  11.8 1.6 copy-start.4
  13.4 1.8 copy-start.8
  13.4 1.8 copy-start.17
  15.3 3.8 copy-start.23
  16.5 147.9 %copy-start.19 = (bf16[16,512]{1,0:T(8,128)(2,1)S(1)}, bf16[16,512]{1,0:T(8,128)(2,1)}, u32[]{:S(2)}) copy-start(bf16[16,512]{1,0:T(8,128)(2,1)} %param.13) | copy-start | bytes 49156
  16.5 213.4 %all-gather.5.cloned.1.call-start = ((), (), s32[]{:S(2)}) async-start(), calls=%async_computation.6 | async-start | bytes 1064960 | tf_op jit(solution)/shard_map/all_gather | solution.py:45
  17.8 509.9 %reduce-scatter.16.cloned.1.call-start = ((), (), s32[]{:S(2)}) async-start(), calls=%async_computation.7 | async-start | bytes 4259840
  161.8 68.1 %copy-start.22 = (pred[16]{0:T(512)(128)(4,1)}, pred[16]{0:T(512)(128)(4,1)S(1)}, u32[]{:S(2)}) copy-start(pred[16]{0:T(512)(128)(4,1)S(1)} %iota_compare_fusion.8) | copy-start | bytes 52
  162.4 2.0 copy-start.15
  229.9 3.3 copy-start.16
  241.6 586.8 %reduce-scatter.24.cloned.1.call-start = ((), (), s32[]{:S(2)}) async-start(), calls=%async_computation.11 | async-start | bytes 532480
  529.0 1.5 copy-start.7
  529.0 2.1 copy-start.9
  529.0 2.4 copy-start.10
  533.7 582.3 %reduce-scatter.20.cloned.1.call-start = ((), (), s32[]{:S(2)}) async-start(), calls=%async_computation.9 | async-start | bytes 2129920
  537.3 866.5 %reduce-scatter.22.cloned.1.call-start = ((), (), s32[]{:S(2)}) async-start(), calls=%async_computation.10 | async-start | bytes 2129920
  541.0 1150.7 %reduce-scatter.18.cloned.1.call-start = ((), (), s32[]{:S(2)}) async-start(), calls=%async_computation.8 | async-start | bytes 2129920
  544.9 1.4 copy-start.13
  546.3 1.4 copy-start.5
  547.7 1.4 copy-start.14
  (7 other events, 7.2 us)
Sparse Core Ops, SparseCore 0:
  16.6 108.1 all-gather.2
  127.2 102.6 all-gather.4
  241.7 285.9 reduce-scatter.15
  533.8 294.5 reduce-scatter.23
  831.3 284.6 reduce-scatter.19
  1119.1 284.7 reduce-scatter.21
  1406.9 284.7 reduce-scatter.17
where the time goes:
time: 1700 us
  waiting for transfers between devices  1420 us (84%)
  blocking collectives  208 us (12%)
  matrix products  25.2 us (1%)
  local copies, waits for them, and re-layouts  21.8 us (1%)
    unnamed x12, waiting for transfers between devices  1360 us
    unnamed x1, blocking collectives  141 us
    psum x1, blocking collectives, shards(): grad_bytes = lax.psum(dx, 'mp').astype(jnp.bfloat16)  66.6 us
    all_gather x1, waiting for transfers between devices, shards(): lax.all_gather(v_loc, 'seq', axis=0, tiled=True)  64.9 us
  transfers between devices with their start and end apart: 7, of which 6 were waited for; matrix products, arithmetic and copies ran while one was open for 1% of the time, Pallas kernels for 0%

commit v1 on v0

v1 whole, which is shorter than its diff:
```python
import jax
import jax.numpy as jnp
from jax import lax
from jax.experimental import pallas as pl
from jax.experimental.pallas import tpu as pltpu
from jax.sharding import PartitionSpec as P

HD = 128
PM = 16
NH = 4
NM = 4
NS = 64
NE = 32
NC = 8
B = 512
DB = 1024
SLOTS = 1024
QB = 256
SCALE = HD**-0.5
LOG2E = 1.4426950408889634
NEG = -1e30
MARK = 2.0**100
F32 = jnp.float32
BF16 = jnp.bfloat16
MESH = pl.DeviceIdType.MESH


def dot(a, b, dims):
    return lax.dot_general(a, b, (dims, ((), ())), preferred_element_type=F32)


def nn(a, b):
    return dot(a, b, ((1,), (0,)))


def nt(a, b):
    return dot(a, b, ((1,), (1,)))


def tn(a, b):
    return dot(a, b, ((0,), (0,)))


def split(a):
    hi = a.astype(BF16)
    return hi, (a - hi.astype(F32)).astype(BF16)


def pool_softmax(scores, member):
    t = jnp.where(member, scores, NEG)
    peak = jnp.max(t, axis=1, keepdims=True)
    expd = jnp.where(member, jnp.exp(t - peak), 0.0)
    total = jnp.sum(expd, axis=1, keepdims=True)
    return expd / jnp.maximum(total, 1e-30)


def kernel(
    x_hbm, ids_ref, pool_ref, wq_hbm, wk_hbm, wv_hbm, g_ref,
    dx_ref, gq_ref, gk_ref, gv_ref, gs_ref,
    x_v, w_v, wcat, qs, xps, rq, rxp, rp, kc, bias, pt, dst, dqkv, us, ru, gsend, rg, sc_send, rs, a_all,
    in_sem, pool_send, pool_recv, q_send, q_recv, x_send, x_recv, f_send, f_recv, fx_send, fx_recv,
    u_send, u_recv, g_send, g_recv, s_send, s_recv,
):
    me = lax.axis_index("seq")
    m = lax.axis_index("mp")
    e = me // 2
    core = me % 2
    h = e % 4
    c = me // 8
    half = (me % 8) // 4
    sib = 2 * e + 1 - core

    def local(src, dst_, sem):
        cp = pltpu.make_async_copy(src, dst_, sem)
        cp.start()
        return cp

    def remote(src, dst_, ssem, rsem, dev):
        pltpu.make_async_remote_copy(
            src_ref=src, dst_ref=dst_, send_sem=ssem, recv_sem=rsem, device_id=dev, device_id_type=MESH
        ).start()

    def wait(ref, sem):
        pltpu.make_async_copy(ref, ref, sem).wait()

    cpx = local(x_hbm, x_v, in_sem.at[0])
    cpw = [local(w, w_v.at[j], in_sem.at[j + 1]) for j, w in enumerate((wq_hbm, wk_hbm, wv_hbm))]

    barrier = pltpu.get_barrier_semaphore()

    def greet(i, _):
        pl.semaphore_signal(barrier, inc=1, device_id=(lax.rem(me + i, NS), m), device_id_type=MESH)
        return 0

    lax.fori_loop(1, NS, greet, 0)

    def greet_far(i, _):
        far = lax.rem(m + 1 + i // NH, NM)
        pl.semaphore_signal(barrier, inc=1, device_id=(8 * c + 2 * (i % NH) + half, far), device_id_type=MESH)
        return 0

    lax.fori_loop(0, 3 * NH, greet_far, 0)
    for dm in range(1, NM):
        pl.semaphore_signal(barrier, inc=1, device_id=(me, lax.rem(m + dm, NM)), device_id_type=MESH)

    ids = ids_ref[...]
    member = ids == lax.broadcasted_iota(jnp.int32, (PM, B), 0)
    count = jnp.max(ids, axis=1, keepdims=True) + 1
    valid = lax.broadcasted_iota(jnp.int32, (PM, HD), 0) < count

    cpx.wait()
    x = x_v[...]
    scores = nt(pool_ref[...], x)
    a = jnp.concatenate([pool_softmax(scores[i : i + 1], member) for i in range(NH)], axis=0)
    a_hi, a_lo = split(a)
    xp = nn(jnp.concatenate([a_hi, a_lo], axis=0), x)
    xp_hi, xp_lo = split(xp[: NH * PM] + xp[NH * PM :])
    for i in range(NC):
        xps[i] = xp_hi[:, i * HD : (i + 1) * HD]
    xp2 = jnp.concatenate([xp_hi, xp_lo], axis=0)
    for j in range(3):
        cpw[j].wait()
        r = nn(xp2, w_v[j])
        r = r[: NH * PM] + r[NH * PM :]
        for i in range(NH):
            block = r[i * PM : (i + 1) * PM, i * HD : (i + 1) * HD]
            if j == 1:
                block = jnp.where(valid, block, MARK)
            qs[i, :, j * HD : (j + 1) * HD] = block.astype(BF16)
    g = g_ref[...].astype(F32)
    for i in range(NH):
        qs[i, :, 3 * HD :] = jnp.where(valid, g[:, i * HD : (i + 1) * HD], 0.0).astype(BF16)

    pl.semaphore_wait(barrier, NS - 1 + 3 * NH + 3)

    local(qs.at[h], rq.at[e, core], q_recv)
    local(xps.at[c, pl.ds(pl.multiple_of(h * PM, PM), PM)], rxp.at[e, core], x_recv)

    def send_q(i, _):
        to = lax.rem(e + i, NE)
        remote(qs.at[to % 4], rq.at[e, core], q_send, q_recv, (2 * to + core, m))
        return 0

    lax.fori_loop(1, NE, send_q, 0)

    def send_x(i, _):
        to = lax.rem(e + i, NE)
        src = xps.at[to // 4, pl.ds(pl.multiple_of((to % 4) * PM, PM), PM)]
        remote(src, rxp.at[e, core], x_send, x_recv, (2 * to + core, m))
        return 0

    lax.fori_loop(1, NE, send_x, 0)

    rp[m] = pool_ref[...]
    for dm in range(1, NM):
        remote(pool_ref, rp.at[m], pool_send.at[dm - 1], pool_recv.at[dm - 1], (me, lax.rem(m + dm, NM)))

    col = pl.ds(pl.multiple_of(h * HD, HD), HD)
    for j in range(3):
        wcat[:, j * HD : (j + 1) * HD] = w_v[j, :, col]

    wait(rq.at[:, core], q_recv)
    remote(rq.at[:, core], rq.at[:, core], f_send, f_recv, (sib, m))
    wait(rxp.at[:, core], x_recv)
    remote(rxp.at[:, core], rxp.at[:, core], fx_send, fx_recv, (sib, m))
    wait(rq.at[:, 1 - core], f_recv)

    k_raw = rq[:, :, :, HD : 2 * HD].reshape(SLOTS, HD).astype(F32)
    bad = k_raw > 0.5 * MARK
    kc[...] = jnp.where(bad, 0.0, k_raw).astype(BF16)
    bias[...] = jnp.where(bad, NEG, 0.0)

    def rows(lane, lo, hi):
        return rq[lo // 32 : hi // 32, :, :, lane * HD : (lane + 1) * HD].reshape(hi - lo, HD)

    for i in reversed(range(SLOTS // QB)):
        lo, n = i * QB, (i + 1) * QB
        q_i, g_i = rows(0, lo, n), rows(3, lo, n)
        t = nt(kc[:n], q_i) * (SCALE * LOG2E)
        b_n = bias[:n]
        t = t + jnp.concatenate([b_n] * (QB // HD), axis=1)
        seen = lax.broadcasted_iota(jnp.int32, (QB, QB), 0) <= lax.broadcasted_iota(jnp.int32, (QB, QB), 1)
        diag = jnp.where(seen, t[lo:], NEG)
        t = diag if i == 0 else jnp.concatenate([t[:lo], diag], axis=0)
        p = jnp.exp2(t - jnp.max(t, axis=0, keepdims=True))
        p = p * (1.0 / jnp.sum(p, axis=0, keepdims=True))
        pb = p.astype(BF16)
        pt[:n, lo:n] = pb
        dp = nt(rows(2, 0, n), g_i)
        delta = jnp.sum(pb.astype(F32) * dp, axis=0, keepdims=True)
        ds = (p * (dp - delta) * SCALE).astype(BF16)
        dst[:n, lo:n] = ds
        dqkv[lo:n, :HD] = tn(ds, kc[:n]).astype(BF16)
    for j in range(SLOTS // QB):
        lo = j * QB
        dqkv[lo : lo + QB, HD : 2 * HD] = nn(dst[lo : lo + QB, lo:], rows(0, lo, SLOTS)).astype(BF16)
        dqkv[lo : lo + QB, 2 * HD :] = nn(pt[lo : lo + QB, lo:], rows(3, lo, SLOTS)).astype(BF16)

    mine = dqkv[pl.ds(pl.multiple_of(8 * PM * c + 4 * PM * core, 4 * PM), 4 * PM), :]
    u = nt(mine, wcat[...]).astype(BF16)
    for t in range(4):
        us[t] = u[t * PM : (t + 1) * PM]
    owner0 = 8 * c + 4 * core

    for dm in range(NM):
        for t in range(4):
            if dm == 0:

                @pl.when(owner0 + t == me)
                def _():
                    local(us.at[t], ru.at[NH * m + h], u_recv.at[m])

                @pl.when(owner0 + t != me)
                def _():
                    remote(us.at[t], ru.at[NH * m + h], u_send, u_recv.at[m], (owner0 + t, m))
            else:
                remote(us.at[t], ru.at[NH * m + h], u_send, u_recv.at[m], (owner0 + t, lax.rem(m + dm, NM)))

    wait(rxp.at[:, 1 - core], fx_recv)
    gsend[...] = tn(rxp[...].reshape(SLOTS, HD), dqkv[...])
    for t in range(4):
        src = gsend.at[pl.ds(pl.multiple_of(4 * PM * core + t * PM, PM), PM)]

        @pl.when(owner0 + t == me)
        def _():
            local(src, rg.at[h], g_recv)

        @pl.when(owner0 + t != me)
        def _():
            remote(src, rg.at[h], g_send, g_recv, (owner0 + t, m))

    for dm in range(1, NM):
        wait(rp.at[0], pool_recv.at[dm - 1])
    rp_all = rp[...].reshape(NM * PM, DB)
    sc_all = nt(rp_all, x)
    for i in range(NM * NH):
        row = (i // NH) * PM + i % NH
        a_all[i * PM : (i + 1) * PM] = pool_softmax(sc_all[row : row + 1], member)

    wait(ru.at[pl.ds(0, NH)], u_recv.at[m])
    u_own = ru[pl.ds(pl.multiple_of(NH * m, NH), NH)].reshape(NH * PM, DB)

    def score_grad(uu, aa):
        ad = aa * nt(uu, x)
        s = jnp.sum(ad, axis=1, keepdims=True)
        d = ad - aa * s
        heads = aa.shape[0] // PM
        pad = jnp.zeros((PM - NH, B), F32)
        out = []
        for i in range(heads):
            out.append(jnp.sum(d[i * PM : (i + 1) * PM], axis=0, keepdims=True))
            if i % NH == NH - 1:
                out.append(pad)
        return jnp.concatenate(out, axis=0).astype(BF16)

    part = nn(score_grad(u_own, a), x)
    for i in range(NC):
        sc_send[i] = part[:8, i * HD : (i + 1) * HD]
    local(sc_send.at[c], rs.at[me], s_recv)

    def send_s(i, _):
        to = lax.rem(me + i, NS)
        remote(sc_send.at[to // 8], rs.at[me], s_send, s_recv, (to, m))
        return 0

    lax.fori_loop(1, NS, send_s, 0)

    for dm in range(1, NM):
        wait(ru.at[pl.ds(0, NH)], u_recv.at[lax.rem(m + dm, NM)])
    u_all = ru[...].reshape(NM * NH * PM, DB)
    aa = a_all[...]
    ds_all = score_grad(u_all, aa)
    left = jnp.concatenate([aa.astype(BF16), ds_all], axis=0)
    right = jnp.concatenate([u_all, rp_all], axis=0)
    dx_ref[...] = tn(left, right).astype(BF16)

    wait(rg, g_recv)
    for i in range(NH):
        for j, ref in enumerate((gq_ref, gk_ref, gv_ref)):
            ref[:, i * HD : (i + 1) * HD] = rg[i, :, j * HD : (j + 1) * HD]
    wait(rs, s_recv)
    tot = jnp.sum(rs[...], axis=0)
    tot = pltpu.roll(tot, lax.rem(HD - PM * (me % 8), HD), 1)
    gs_ref[...] = tot[:NH, :PM]

    for dm in range(1, NM):
        wait(pool_ref, pool_send.at[dm - 1])
    wait(rq.at[pl.ds(0, NE - 1), 0], q_send)
    wait(rxp.at[pl.ds(0, NE - 1), 0], x_send)
    wait(rq.at[:, 0], f_send)
    wait(rxp.at[:, 0], fx_send)
    own = half == core

    @pl.when(own)
    def _():
        wait(ru.at[pl.ds(0, 15)], u_send)
        wait(rg.at[pl.ds(0, 3)], g_send)

    @pl.when(jnp.logical_not(own))
    def _():
        wait(ru, u_send)
        wait(rg, g_send)

    wait(rs.at[pl.ds(0, NS - 1)], s_send)


def shards(byte_states, byte_patch, pool_score, w_query, w_key, w_value, out_grad):
    pool = jnp.pad(pool_score.T, ((0, PM - NH), (0, 0)))
    vmem = pl.BlockSpec(memory_space=pltpu.VMEM)
    hbm = pl.BlockSpec(memory_space=pl.ANY)
    dma = pltpu.SemaphoreType.DMA
    dx, gq, gk, gv, gs = pl.pallas_call(
        kernel,
        out_shape=(
            jax.ShapeDtypeStruct((B, DB), BF16),
            jax.ShapeDtypeStruct((PM, NH * HD), F32),
            jax.ShapeDtypeStruct((PM, NH * HD), F32),
            jax.ShapeDtypeStruct((PM, NH * HD), F32),
            jax.ShapeDtypeStruct((NH, PM), F32),
        ),
        in_specs=[hbm, vmem, vmem, hbm, hbm, hbm, vmem],
        out_specs=(vmem,) * 5,
        scratch_shapes=[
            pltpu.VMEM((B, DB), BF16),
            pltpu.VMEM((3, DB, NH * HD), BF16),
            pltpu.VMEM((DB, 3 * HD), BF16),
            pltpu.VMEM((NH, PM, 4 * HD), BF16),
            pltpu.VMEM((NC, NH * PM, HD), BF16),
            pltpu.VMEM((NE, 2, PM, 4 * HD), BF16),
            pltpu.VMEM((NE, 2, PM, HD), BF16),
            pltpu.VMEM((NM, PM, DB), BF16),
            pltpu.VMEM((SLOTS, HD), BF16),
            pltpu.VMEM((SLOTS, HD), F32),
            pltpu.VMEM((SLOTS, SLOTS), BF16),
            pltpu.VMEM((SLOTS, SLOTS), BF16),
            pltpu.VMEM((SLOTS, 3 * HD), BF16),
            pltpu.VMEM((4, PM, DB), BF16),
            pltpu.VMEM((NM * NH, PM, DB), BF16),
            pltpu.VMEM((HD, 3 * HD), F32),
            pltpu.VMEM((NH, PM, 3 * HD), F32),
            pltpu.VMEM((NC, 8, HD), F32),
            pltpu.VMEM((NS, 8, HD), F32),
            pltpu.VMEM((NM * NH * PM, B), F32),
            dma((4,)),
            dma((3,)), dma((3,)),
            dma, dma,
            dma, dma,
            dma, dma,
            dma, dma,
            dma, dma((NM,)),
            dma, dma,
            dma, dma,
        ],
        compiler_params=pltpu.CompilerParams(
            collective_id=0, has_side_effects=True, vmem_limit_bytes=48 * 1024 * 1024
        ),
    )(byte_states, byte_patch, pool, w_query, w_key, w_value, out_grad)
    return dx, gq, gk, gv, gs.T


def solution(mesh):
    return jax.shard_map(
        shards,
        mesh=mesh,
        in_specs=(
            P("seq", None),
            P("seq", None),
            P(None, "mp"),
            P(None, "mp"),
            P(None, "mp"),
            P(None, "mp"),
            P("seq", "mp"),
        ),
        out_specs=(P("seq", None), P("seq", "mp"), P("seq", "mp"), P("seq", "mp"), P("seq", "mp")),
        check_vma=False,
    )
```

time: 1700 us -> 55.2 us (0.03)
  waiting for transfers between devices: 1420 us -> 0 us
  blocking collectives: 208 us -> 0 us
  Pallas kernels: 0 us -> 45.2 us
  matrix products: 25.2 us -> 0 us
    unnamed x12 -> x0, waiting for transfers between devices: 1360 us -> none
    unnamed x1 -> x0, blocking collectives: 141 us -> none
    psum x1 -> x0, blocking collectives: 66.6 us -> none  [shards(): grad_bytes = lax.psum(dx, 'mp').astype(jnp.bfloat16)]
    all_gather x2 -> x0, waiting for transfers between devices: 65 us -> none  [the longest x1 64.9 us: shards(): lax.all_gather(v_loc, 'seq', axis=0, tiled=True)]
    pallas_call x0 -> x1, Pallas kernels: none -> 45.2 us  [shards(): pl.pallas_call(kernel, out_shape=(jax.ShapeDtypeStruct((B, DB), BF16), ja...]
    dot_general x24 -> x0, matrix products: 25.2 us -> none  [the longest x4 5.5 us: shards(): lax.dot_general(byte_states, dy, (((0,), (0,)), ((), ())), preferred_elem...]
  transfers between devices with their start and end apart: 7 -> 0, of which waited for: 6 -> 0; matrix products, arithmetic and copies ran while one was open for 1% -> 0% of each run, Pallas kernels for 0% -> 0%
where the time goes in v1:
time: 55.2 us; the launch traced here: 54.9 us
  Pallas kernels  45.2 us (82%)
  local copies, waits for them, and re-layouts  9.01 us (16%)
  between operations  0.67 us (1%)
    pallas_call x1, Pallas kernels, shards(): pl.pallas_call(kernel, out_shape=(jax.ShapeDtypeStruct((B, DB), BF16), ja...  45.2 us
    unnamed x17, local copies, waits for them, and re-layouts  8.29 us

profile of v1, /device:TPU:1, one launch (start us, length us, event | category | flops | bytes accessed | tf_op | source)
XLA Modules:
  0.0 54.9 jit_solution(1951108101099304449)
XLA Ops:
  0.6 0.0 copy-start.4
  0.6 0.0 copy-start.5
  0.7 0.7 %pad.4.pool_ref = bf16[16,1024]{1,0:T(8,128)(2,1)S(1)} pad(bf16[4,1024]{1,0:T(4,128)(2,1)} %bitcast.3, bf16[]{:T(256)} %constant.2.clone.1), padding=0_12x0_0 | pad | bytes 40962 | tf_op jit(solution)/shard_map/jit(_pad)/pad | solution.py:308
  1.4 0.0 copy-done.4
  1.4 0.0 copy-done.5
  1.4 0.0 copy-start
  1.4 1.2 %copy-done = bf16[512,1024]{1,0:T(8,128)(2,1)S(1)} copy-done((bf16[512,1024]{1,0:T(8,128)(2,1)S(1)}, bf16[512,1024]{1,0:T(8,128)(2,1)}, u32[]{:S(2)}) %copy-start) | copy-done | bytes 1048600
  2.6 0.0 copy-start.1
  2.6 1.2 %copy-done.1 = bf16[1024,512]{1,0:T(8,128)(2,1)S(1)} copy-done((bf16[1024,512]{1,0:T(8,128)(2,1)S(1)}, bf16[1024,512]{1,0:T(8,128)(2,1)}, u32[]{:S(2)}) %copy-start.1) | copy-done | bytes 1048600
  3.8 0.0 copy-start.2
  3.8 1.2 %copy-done.2 = bf16[1024,512]{1,0:T(8,128)(2,1)S(1)} copy-done((bf16[1024,512]{1,0:T(8,128)(2,1)S(1)}, bf16[1024,512]{1,0:T(8,128)(2,1)}, u32[]{:S(2)}) %copy-start.2) | copy-done | bytes 1048600
  5.1 0.0 copy-start.3
  5.1 1.2 %copy-done.3 = bf16[1024,512]{1,0:T(8,128)(2,1)S(1)} copy-done((bf16[1024,512]{1,0:T(8,128)(2,1)S(1)}, bf16[1024,512]{1,0:T(8,128)(2,1)}, u32[]{:S(2)}) %copy-start.3) | copy-done | bytes 1048600
  6.3 45.2 %shard_map.110 = (bf16[512,1024]{1,0:T(8,128)(2,1)S(1)}, f32[16,512]{1,0:T(8,128)S(1)}, f32[16,512]{1,0:T(8,128)S(1)}, f32[16,512]{1,0:T(8,128)S(1)}, f32[4,16]{1,0:T(4,128)S(1)}) custom-call(bf16[512,1024]{1,0:T(8,128)(2,1)S(1)} %copy-done, s32[1,512]{1,0:T(1,128)S(1)} %copy-done.5, bf16[16,1024]{1,0:T(8,128)(2,1)S(1)} %pad.4.pool_ref, ...), custom_call_target="tpu_custom_call" | custom-call | tf_op jit(solution)/shard_map/pallas_call | solution.py:312
  51.5 1.0 %copy.17 = bf16[512,1024]{1,0:T(8,128)(2,1)} copy(bf16[512,1024]{1,0:T(8,128)(2,1)S(1)} %get-tuple-element.20) | data formatting | bytes 2097152
  52.4 0.6 %copy.18 = f32[16,512]{1,0:T(8,128)} copy(f32[16,512]{1,0:T(8,128)S(1)} %get-tuple-element.21) | data formatting | bytes 65536
  53.1 0.6 %copy.19 = f32[16,512]{1,0:T(8,128)} copy(f32[16,512]{1,0:T(8,128)S(1)} %get-tuple-element.22) | data formatting | bytes 65536
  53.7 0.6 %copy.20 = f32[16,512]{1,0:T(8,128)} copy(f32[16,512]{1,0:T(8,128)S(1)} %get-tuple-element.23) | data formatting | bytes 65536
  54.3 0.6 %copy.21 = f32[16,4]{0,1:T(4,128)} copy(f32[16,4]{0,1:T(4,128)S(1)} %bitcast.2) | data formatting | bytes 512
Async XLA Ops:
  0.6 0.7 %copy-start.4 = (bf16[16,512]{1,0:T(8,128)(2,1)S(1)}, bf16[16,512]{1,0:T(8,128)(2,1)}, u32[]{:S(2)}) copy-start(bf16[16,512]{1,0:T(8,128)(2,1)} %g_ref.1) | copy-start | bytes 49156
  0.6 0.7 %copy-start.5 = (s32[1,512]{1,0:T(1,128)S(1)}, s32[1,512]{1,0:T(1,128)}, u32[]{:S(2)}) copy-start(s32[1,512]{1,0:T(1,128)} %ids_ref.1) | copy-start | bytes 6148
  1.4 1.2 %copy-start = (bf16[512,1024]{1,0:T(8,128)(2,1)S(1)}, bf16[512,1024]{1,0:T(8,128)(2,1)}, u32[]{:S(2)}) copy-start(bf16[512,1024]{1,0:T(8,128)(2,1)} %x_hbm.1) | copy-start | bytes 3145732
  2.6 1.2 %copy-start.1 = (bf16[1024,512]{1,0:T(8,128)(2,1)S(1)}, bf16[1024,512]{1,0:T(8,128)(2,1)}, u32[]{:S(2)}) copy-start(bf16[1024,512]{1,0:T(8,128)(2,1)} %wq_hbm.1) | copy-start | bytes 3145732
  3.8 1.2 %copy-start.2 = (bf16[1024,512]{1,0:T(8,128)(2,1)S(1)}, bf16[1024,512]{1,0:T(8,128)(2,1)}, u32[]{:S(2)}) copy-start(bf16[1024,512]{1,0:T(8,128)(2,1)} %wk_hbm.1) | copy-start | bytes 3145732
  5.1 1.2 %copy-start.3 = (bf16[1024,512]{1,0:T(8,128)(2,1)S(1)}, bf16[1024,512]{1,0:T(8,128)(2,1)}, u32[]{:S(2)}) copy-start(bf16[1024,512]{1,0:T(8,128)(2,1)} %wv_hbm.1) | copy-start | bytes 3145732

commit v2 on v1

--- a/solution.py
+++ b/solution.py
@@ -11,6 +11,7 @@
 NM = 4
 NS = 64
 NE = 32
+EMIT = 8
 NC = 8
 B = 512
 DB = 1024
@@ -23,6 +24,10 @@
 F32 = jnp.float32
 BF16 = jnp.bfloat16
 MESH = pl.DeviceIdType.MESH
+OFFS = sorted(
+    ((dx, dy, dz) for dz in range(2) for dy in range(4) for dx in range(4) if dx or dy or dz),
+    key=lambda o: (-(min(o[0], 4 - o[0]) + min(o[1], 4 - o[1]) + o[2]), o),
+)
 
 
 def dot(a, b, dims):
@@ -56,10 +61,10 @@
 
 def kernel(
     x_hbm, ids_ref, pool_ref, wq_hbm, wk_hbm, wv_hbm, g_ref,
-    dx_ref, gq_ref, gk_ref, gv_ref, gs_ref,
-    x_v, w_v, wcat, qs, xps, rq, rxp, rp, kc, bias, pt, dst, dqkv, us, ru, gsend, rg, sc_send, rs, a_all,
+    dx_hbm, gw_hbm, gs_hbm,
+    x_v, w_v, wcat, pool_v, qs, xps, rq, rxp, rp, kc, bias, pt, dst, dqkv, us, ru, gsend, rg, sc_send, rs, tot_send, rt, a_all, acc, dx_v, gw_v, gs_v,
     in_sem, pool_send, pool_recv, q_send, q_recv, x_send, x_recv, f_send, f_recv, fx_send, fx_recv,
-    u_send, u_recv, g_send, g_recv, s_send, s_recv,
+    u_send, u_recv, v_send, g_send, g_recv, s_send, s_recv, t_send, t_recv, out_sem,
 ):
     me = lax.axis_index("seq")
     m = lax.axis_index("mp")
@@ -86,22 +91,26 @@
     cpx = local(x_hbm, x_v, in_sem.at[0])
     cpw = [local(w, w_v.at[j], in_sem.at[j + 1]) for j, w in enumerate((wq_hbm, wk_hbm, wv_hbm))]
 
+    def chip(off):
+        z, y, xx = e // 16, (e // 4) % 4, e % 4
+        return lax.rem(z + off[2], 2) * 16 + lax.rem(y + off[1], 4) * 4 + lax.rem(xx + off[0], 4)
+
     barrier = pltpu.get_barrier_semaphore()
 
-    def greet(i, _):
-        pl.semaphore_signal(barrier, inc=1, device_id=(lax.rem(me + i, NS), m), device_id_type=MESH)
-        return 0
-
-    lax.fori_loop(1, NS, greet, 0)
-
-    def greet_far(i, _):
-        far = lax.rem(m + 1 + i // NH, NM)
-        pl.semaphore_signal(barrier, inc=1, device_id=(8 * c + 2 * (i % NH) + half, far), device_id_type=MESH)
-        return 0
-
-    lax.fori_loop(0, 3 * NH, greet_far, 0)
+    def greet(dev):
+        pl.semaphore_signal(barrier, inc=1, device_id=dev, device_id_type=MESH)
+
+    for off in OFFS:
+        greet((2 * chip(off) + core, m))
+    ahead, behind = lax.rem(m + 1, NM), lax.rem(m + 3, NM)
+    for far in (ahead, behind):
+        for i in range(NH):
+            greet((8 * c + 2 * i + half, far))
     for dm in range(1, NM):
-        pl.semaphore_signal(barrier, inc=1, device_id=(me, lax.rem(m + dm, NM)), device_id_type=MESH)
+        greet((me, lax.rem(m + dm, NM)))
+    for i in range(1, NH):
+        greet((8 * c + 2 * lax.rem(h + i, NH) + 1 - core, m))
+    greet((sib, m))
 
     ids = ids_ref[...]
     member = ids == lax.broadcasted_iota(jnp.int32, (PM, B), 0)
@@ -110,7 +119,8 @@
 
     cpx.wait()
     x = x_v[...]
-    scores = nt(pool_ref[...], x)
+    pool_v[...] = jnp.concatenate([pool_ref[...].astype(F32), jnp.zeros((PM - NH, DB), F32)], axis=0).astype(BF16)
+    scores = nt(pool_v[...], x)
     a = jnp.concatenate([pool_softmax(scores[i : i + 1], member) for i in range(NH)], axis=0)
     a_hi, a_lo = split(a)
     xp = nn(jnp.concatenate([a_hi, a_lo], axis=0), x)
@@ -131,17 +141,14 @@
     for i in range(NH):
         qs[i, :, 3 * HD :] = jnp.where(valid, g[:, i * HD : (i + 1) * HD], 0.0).astype(BF16)
 
-    pl.semaphore_wait(barrier, NS - 1 + 3 * NH + 3)
+    pl.semaphore_wait(barrier, len(OFFS) + 2 * NH + 3 + 3 + 1)
 
     local(qs.at[h], rq.at[e, core], q_recv)
     local(xps.at[c, pl.ds(pl.multiple_of(h * PM, PM), PM)], rxp.at[e, core], x_recv)
 
-    def send_q(i, _):
-        to = lax.rem(e + i, NE)
+    for off in OFFS:
+        to = chip(off)
         remote(qs.at[to % 4], rq.at[e, core], q_send, q_recv, (2 * to + core, m))
-        return 0
-
-    lax.fori_loop(1, NE, send_q, 0)
 
     def send_x(i, _):
         to = lax.rem(e + i, NE)
@@ -151,9 +158,9 @@
 
     lax.fori_loop(1, NE, send_x, 0)
 
-    rp[m] = pool_ref[...]
+    rp[m] = pool_v[...]
     for dm in range(1, NM):
-        remote(pool_ref, rp.at[m], pool_send.at[dm - 1], pool_recv.at[dm - 1], (me, lax.rem(m + dm, NM)))
+        remote(pool_v, rp.at[m], pool_send.at[dm - 1], pool_recv.at[dm - 1], (me, lax.rem(m + dm, NM)))
 
     col = pl.ds(pl.multiple_of(h * HD, HD), HD)
     for j in range(3):
@@ -202,19 +209,29 @@
         us[t] = u[t * PM : (t + 1) * PM]
     owner0 = 8 * c + 4 * core
 
-    for dm in range(NM):
+    def send_u(far):
         for t in range(4):
-            if dm == 0:
-
-                @pl.when(owner0 + t == me)
-                def _():
-                    local(us.at[t], ru.at[NH * m + h], u_recv.at[m])
-
-                @pl.when(owner0 + t != me)
-                def _():
-                    remote(us.at[t], ru.at[NH * m + h], u_send, u_recv.at[m], (owner0 + t, m))
-            else:
-                remote(us.at[t], ru.at[NH * m + h], u_send, u_recv.at[m], (owner0 + t, lax.rem(m + dm, NM)))
+            remote(us.at[t], ru.at[NH * m + h], u_send, u_recv.at[m, h // 2], (owner0 + t, far))
+
+    @pl.when(h < 2)
+    def _():
+        send_u(ahead)
+        send_u(behind)
+
+    @pl.when(h >= 2)
+    def _():
+        send_u(behind)
+        send_u(ahead)
+
+    for t in range(4):
+
+        @pl.when(owner0 + t == me)
+        def _():
+            local(us.at[t], ru.at[NH * m + h], u_recv.at[m, h // 2])
+
+        @pl.when(owner0 + t != me)
+        def _():
+            remote(us.at[t], ru.at[NH * m + h], u_send, u_recv.at[m, h // 2], (owner0 + t, m))
 
     wait(rxp.at[:, 1 - core], fx_recv)
     gsend[...] = tn(rxp[...].reshape(SLOTS, HD), dqkv[...])
@@ -237,93 +254,148 @@
         row = (i // NH) * PM + i % NH
         a_all[i * PM : (i + 1) * PM] = pool_softmax(sc_all[row : row + 1], member)
 
-    wait(ru.at[pl.ds(0, NH)], u_recv.at[m])
-    u_own = ru[pl.ds(pl.multiple_of(NH * m, NH), NH)].reshape(NH * PM, DB)
-
-    def score_grad(uu, aa):
-        ad = aa * nt(uu, x)
-        s = jnp.sum(ad, axis=1, keepdims=True)
-        d = ad - aa * s
-        heads = aa.shape[0] // PM
-        pad = jnp.zeros((PM - NH, B), F32)
-        out = []
-        for i in range(heads):
-            out.append(jnp.sum(d[i * PM : (i + 1) * PM], axis=0, keepdims=True))
-            if i % NH == NH - 1:
-                out.append(pad)
-        return jnp.concatenate(out, axis=0).astype(BF16)
-
-    part = nn(score_grad(u_own, a), x)
+    def heads(group, first, n):
+        return pl.ds(NH * group + first, n)
+
+    def arrived(group, part):
+        wait(ru.at[pl.ds(0, 2)], u_recv.at[group, part])
+
+    def group_of(group):
+        u_g = ru[heads(group, 0, NH)].reshape(NH * PM, DB)
+        a_g = a_all[pl.ds(pl.multiple_of(NH * PM * group, NH * PM), NH * PM), :]
+        ad = a_g * nt(u_g, x)
+        d = ad - a_g * jnp.sum(ad, axis=1, keepdims=True)
+        rows_ = [jnp.sum(d[i * PM : (i + 1) * PM], axis=0, keepdims=True) for i in range(NH)]
+        ds_g = jnp.concatenate(rows_ + [jnp.zeros((PM - NH, B), F32)], axis=0).astype(BF16)
+        left = jnp.concatenate([a_g.astype(BF16), ds_g], axis=0)
+        return ds_g, left, jnp.concatenate([u_g, rp[group]], axis=0)
+
+    arrived(m, 0)
+    arrived(m, 1)
+    ds_own, left, right = group_of(m)
+    part = nn(ds_own, x)
     for i in range(NC):
         sc_send[i] = part[:8, i * HD : (i + 1) * HD]
-    local(sc_send.at[c], rs.at[me], s_recv)
+    local(sc_send.at[c], rs.at[c], s_recv)
 
     def send_s(i, _):
-        to = lax.rem(me + i, NS)
-        remote(sc_send.at[to // 8], rs.at[me], s_send, s_recv, (to, m))
+        to = lax.rem(c + i, NC)
+        remote(sc_send.at[to], rs.at[c], s_send, s_recv, (8 * to + me % 8, m))
         return 0
 
-    lax.fori_loop(1, NS, send_s, 0)
-
-    for dm in range(1, NM):
-        wait(ru.at[pl.ds(0, NH)], u_recv.at[lax.rem(m + dm, NM)])
-    u_all = ru[...].reshape(NM * NH * PM, DB)
-    aa = a_all[...]
-    ds_all = score_grad(u_all, aa)
-    left = jnp.concatenate([aa.astype(BF16), ds_all], axis=0)
-    right = jnp.concatenate([u_all, rp_all], axis=0)
-    dx_ref[...] = tn(left, right).astype(BF16)
+    lax.fori_loop(1, NC, send_s, 0)
+
+    opposite = lax.rem(m + 2, NM)
+    arrived(behind, 0)
+    remote(ru.at[heads(behind, 0, 2)], ru.at[heads(behind, 0, 2)], v_send.at[0], u_recv.at[behind, 0], (me, ahead))
+    arrived(ahead, 1)
+    remote(ru.at[heads(ahead, 2, 2)], ru.at[heads(ahead, 2, 2)], v_send.at[1], u_recv.at[ahead, 1], (me, behind))
+
+    acc[...] = tn(left, right)
+
+    wait(rs, s_recv)
+    tot_send[...] = jnp.sum(rs[...], axis=0)
+    local(tot_send, rt.at[me % 8], t_recv)
+
+    def send_t(i, _):
+        remote(tot_send, rt.at[me % 8], t_send, t_recv, (8 * c + lax.rem(me % 8 + i, 8), m))
+        return 0
+
+    lax.fori_loop(1, 8, send_t, 0)
+
+    arrived(behind, 1)
+    _, left, right = group_of(behind)
+    acc[...] += tn(left, right)
+    arrived(ahead, 0)
+    _, left, right = group_of(ahead)
+    acc[...] += tn(left, right)
 
     wait(rg, g_recv)
     for i in range(NH):
-        for j, ref in enumerate((gq_ref, gk_ref, gv_ref)):
-            ref[:, i * HD : (i + 1) * HD] = rg[i, :, j * HD : (j + 1) * HD]
-    wait(rs, s_recv)
-    tot = jnp.sum(rs[...], axis=0)
+        for j in range(3):
+            gw_v[j, :, i * HD : (i + 1) * HD] = rg[i, :, j * HD : (j + 1) * HD]
+    out_w = local(gw_v, gw_hbm, out_sem.at[0])
+    wait(rt, t_recv)
+    tot = jnp.sum(rt[...], axis=0)
     tot = pltpu.roll(tot, lax.rem(HD - PM * (me % 8), HD), 1)
-    gs_ref[...] = tot[:NH, :PM]
+    gs_v[...] = tot[:NH, :PM]
+    out_s = local(gs_v, gs_hbm, out_sem.at[1])
+
+    arrived(opposite, 0)
+    arrived(opposite, 1)
+    _, left, right = group_of(opposite)
+    out_x = []
+    step = B // 4
+    for i in range(4):
+        at = pl.ds(i * step, step)
+        dx_v[at, :] = (acc[at, :] + tn(left[:, i * step : (i + 1) * step], right)).astype(BF16)
+        out_x.append(local(dx_v.at[at], dx_hbm.at[at], out_sem.at[2 + i]))
 
     for dm in range(1, NM):
-        wait(pool_ref, pool_send.at[dm - 1])
+        wait(pool_v, pool_send.at[dm - 1])
     wait(rq.at[pl.ds(0, NE - 1), 0], q_send)
     wait(rxp.at[pl.ds(0, NE - 1), 0], x_send)
     wait(rq.at[:, 0], f_send)
     wait(rxp.at[:, 0], fx_send)
+    wait(ru.at[pl.ds(0, 2)], v_send.at[0])
+    wait(ru.at[pl.ds(0, 2)], v_send.at[1])
     own = half == core
 
     @pl.when(own)
     def _():
-        wait(ru.at[pl.ds(0, 15)], u_send)
+        wait(ru.at[pl.ds(0, 11)], u_send)
         wait(rg.at[pl.ds(0, 3)], g_send)
 
     @pl.when(jnp.logical_not(own))
     def _():
-        wait(ru, u_send)
+        wait(ru.at[pl.ds(0, 12)], u_send)
         wait(rg, g_send)
 
-    wait(rs.at[pl.ds(0, NS - 1)], s_send)
+    wait(rs.at[pl.ds(0, NC - 1)], s_send)
+    wait(rt.at[pl.ds(0, 7)], t_send)
+    for cp in [out_w, out_s] + out_x:
+        cp.wait()
+
+
+def emit(dx_in, gw_in, gs_in, dx_out, gq_out, gk_out, gv_out, gs_out, dx_v, gw_v, gs_v, in_sem, out_sem):
+    step = B // EMIT
+    ins, outs = [], []
+    for i in range(EMIT):
+        at = pl.ds(i * step, step)
+        ins.append(pltpu.make_async_copy(dx_in.at[at], dx_v.at[at], in_sem.at[i]))
+        outs.append(pltpu.make_async_copy(dx_v.at[at], dx_out.at[at], out_sem.at[i]))
+    for i, ref in enumerate((gq_out, gk_out, gv_out)):
+        ins.append(pltpu.make_async_copy(gw_in.at[i], gw_v.at[i], in_sem.at[EMIT + i]))
+        outs.append(pltpu.make_async_copy(gw_v.at[i], ref, out_sem.at[EMIT + i]))
+    ins.append(pltpu.make_async_copy(gs_in, gs_v, in_sem.at[EMIT + 3]))
+    outs.append(pltpu.make_async_copy(gs_v, gs_out, out_sem.at[EMIT + 3]))
+    for cp in ins:
+        cp.start()
+    for got, cp in zip(ins, outs):
+        got.wait()
+        cp.start()
+    for cp in outs:
+        cp.wait()
 
 
 def shards(byte_states, byte_patch, pool_score, w_query, w_key, w_value, out_grad):
-    pool = jnp.pad(pool_score.T, ((0, PM - NH), (0, 0)))
+    pool = pool_score.T
     vmem = pl.BlockSpec(memory_space=pltpu.VMEM)
-    hbm = pl.BlockSpec(memory_space=pl.ANY)
+    anyspace = pl.BlockSpec(memory_space=pl.ANY)
     dma = pltpu.SemaphoreType.DMA
-    dx, gq, gk, gv, gs = pl.pallas_call(
+    x_shape = jax.ShapeDtypeStruct((B, DB), BF16)
+    w_shape = jax.ShapeDtypeStruct((PM, NH * HD), F32)
+    s_shape = jax.ShapeDtypeStruct((NH, PM), F32)
+    made = pl.pallas_call(
         kernel,
-        out_shape=(
-            jax.ShapeDtypeStruct((B, DB), BF16),
-            jax.ShapeDtypeStruct((PM, NH * HD), F32),
-            jax.ShapeDtypeStruct((PM, NH * HD), F32),
-            jax.ShapeDtypeStruct((PM, NH * HD), F32),
-            jax.ShapeDtypeStruct((NH, PM), F32),
-        ),
-        in_specs=[hbm, vmem, vmem, hbm, hbm, hbm, vmem],
-        out_specs=(vmem,) * 5,
+        out_shape=(x_shape, jax.ShapeDtypeStruct((3, PM, NH * HD), F32), s_shape),
+        in_specs=[anyspace, vmem, vmem, anyspace, anyspace, anyspace, vmem],
+        out_specs=(anyspace,) * 3,
         scratch_shapes=[
             pltpu.VMEM((B, DB), BF16),
             pltpu.VMEM((3, DB, NH * HD), BF16),
             pltpu.VMEM((DB, 3 * HD), BF16),
+            pltpu.VMEM((PM, DB), BF16),
             pltpu.VMEM((NH, PM, 4 * HD), BF16),
             pltpu.VMEM((NC, NH * PM, HD), BF16),
             pltpu.VMEM((NE, 2, PM, 4 * HD), BF16),
@@ -339,22 +411,45 @@
             pltpu.VMEM((HD, 3 * HD), F32),
             pltpu.VMEM((NH, PM, 3 * HD), F32),
             pltpu.VMEM((NC, 8, HD), F32),
-            pltpu.VMEM((NS, 8, HD), F32),
+            pltpu.VMEM((NC, 8, HD), F32),
+            pltpu.VMEM((8, HD), F32),
+            pltpu.VMEM((8, 8, HD), F32),
             pltpu.VMEM((NM * NH * PM, B), F32),
+            pltpu.VMEM((B, DB), F32),
+            pltpu.VMEM((B, DB), BF16),
+            pltpu.VMEM((3, PM, NH * HD), F32),
+            pltpu.VMEM((NH, PM), F32),
             dma((4,)),
             dma((3,)), dma((3,)),
             dma, dma,
             dma, dma,
             dma, dma,
             dma, dma,
-            dma, dma((NM,)),
-            dma, dma,
-            dma, dma,
+            dma, dma((NM, 2)),
+            dma((2,)),
+            dma, dma,
+            dma, dma,
+            dma, dma,
+            dma((6,)),
         ],
         compiler_params=pltpu.CompilerParams(
-            collective_id=0, has_side_effects=True, vmem_limit_bytes=48 * 1024 * 1024
+            collective_id=0, has_side_effects=True, vmem_limit_bytes=61 * 1024 * 1024
         ),
     )(byte_states, byte_patch, pool, w_query, w_key, w_value, out_grad)
+    dx, gq, gk, gv, gs = pl.pallas_call(
+        emit,
+        out_shape=(x_shape, w_shape, w_shape, w_shape, s_shape),
+        in_specs=[anyspace] * 3,
+        out_specs=(anyspace,) * 5,
+        scratch_shapes=[
+            pltpu.VMEM((B, DB), BF16),
+            pltpu.VMEM((3, PM, NH * HD), F32),
+            pltpu.VMEM((NH, PM), F32),
+            dma((EMIT + 4,)),
+            dma((EMIT + 4,)),
+        ],
+        compiler_params=pltpu.CompilerParams(vmem_limit_bytes=61 * 1024 * 1024),
+    )(*made)
     return dx, gq, gk, gv, gs.T
 
 

time: 55.2 us -> 46.5 us (0.84)
  local copies, waits for them, and re-layouts: 9.01 us -> 0 us
    unnamed x17 -> x0, local copies, waits for them, and re-layouts: 8.29 us -> none
    pad x1 -> x0, local copies, waits for them, and re-layouts: 0.71 us -> none  [shards(): pool = jnp.pad(pool_score.T, ((0, PM - NH), (0, 0)))]
    pallas_call x1 -> x2, Pallas kernels: 45.2 us -> 45.6 us  [the longest x1 43.4 us: shards(): pl.pallas_call(kernel, out_shape=(x_shape, jax.ShapeDtypeStruct((3, PM, N...]
where the time goes in v2:
time: 46.5 us; the launch traced here: 46.3 us
  Pallas kernels  45.6 us (98%)
  between operations  0.64 us (1%)
    pallas_call x1, Pallas kernels, shards(): pl.pallas_call(kernel, out_shape=(x_shape, jax.ShapeDtypeStruct((3, PM, N...  43.4 us
    pallas_call x1, Pallas kernels, shards(): pl.pallas_call(emit, out_shape=(x_shape, w_shape, w_shape, w_shape, s_sha...  2.18 us

profile of v2, /device:TPU:1, one launch (start us, length us, event | category | flops | bytes accessed | tf_op | source)
XLA Modules:
  0.0 46.3 jit_solution(10574343237202261890)
XLA Ops:
  0.6 43.4 %shard_map.110 = (bf16[512,1024]{1,0:T(8,128)(2,1)}, f32[3,16,512]{2,1,0:T(8,128)}, f32[4,16]{1,0:T(4,128)}) custom-call(bf16[512,1024]{1,0:T(8,128)(2,1)} %x_hbm.1, s32[1,512]{1,0:T(1,128)} %ids_ref.1, bf16[4,1024]{1,0:T(4,128)(2,1)} %bitcast.2, bf16[1024,512]{1,0:T(8,128)(2,1)} %wq_hbm.1, bf16[1024,512]{1,0:T(8,128)(2,1)} %wk_hbm.1, ...), custom_call_target="tpu_custom_call" | custom-call | tf_op jit(solution)/shard_map/pallas_call | solution.py:389
  44.1 2.2 %shard_map.111 = (bf16[512,1024]{1,0:T(8,128)(2,1)}, f32[16,512]{1,0:T(8,128)}, f32[16,512]{1,0:T(8,128)}, f32[16,512]{1,0:T(8,128)}, f32[4,16]{1,0:T(4,128)}) custom-call(bf16[512,1024]{1,0:T(8,128)(2,1)} %get-tuple-element.13.dx_in, f32[3,16,512]{2,1,0:T(8,128)} %get-tuple-element.14.gw_in, f32[4,16]{1,0:T(4,128)} %get-tuple-element.15.gs_in), custom_call_target="tpu_custom_call" | custom-call | tf_op jit(solution)/shard_map/pallas_call | solution.py:439

commit v3 on v2

--- a/solution.py
+++ b/solution.py
@@ -164,18 +164,17 @@
 
     col = pl.ds(pl.multiple_of(h * HD, HD), HD)
     for j in range(3):
-        wcat[:, j * HD : (j + 1) * HD] = w_v[j, :, col]
+        wcat[j * HD : (j + 1) * HD, :] = w_v[j, :, col].T
 
     wait(rq.at[:, core], q_recv)
     remote(rq.at[:, core], rq.at[:, core], f_send, f_recv, (sib, m))
-    wait(rxp.at[:, core], x_recv)
-    remote(rxp.at[:, core], rxp.at[:, core], fx_send, fx_recv, (sib, m))
     wait(rq.at[:, 1 - core], f_recv)
 
     k_raw = rq[:, :, :, HD : 2 * HD].reshape(SLOTS, HD).astype(F32)
     bad = k_raw > 0.5 * MARK
     kc[...] = jnp.where(bad, 0.0, k_raw).astype(BF16)
     bias[...] = jnp.where(bad, NEG, 0.0)
+    k_t = kc[...].T
 
     def rows(lane, lo, hi):
         return rq[lo // 32 : hi // 32, :, :, lane * HD : (lane + 1) * HD].reshape(hi - lo, HD)
@@ -197,21 +196,33 @@
         delta = jnp.sum(pb.astype(F32) * dp, axis=0, keepdims=True)
         ds = (p * (dp - delta) * SCALE).astype(BF16)
         dst[:n, lo:n] = ds
-        dqkv[lo:n, :HD] = tn(ds, kc[:n]).astype(BF16)
+        dqkv[lo:n, :HD] = nn(k_t[:, :n], ds).T.astype(BF16)
     for j in range(SLOTS // QB):
         lo = j * QB
         dqkv[lo : lo + QB, HD : 2 * HD] = nn(dst[lo : lo + QB, lo:], rows(0, lo, SLOTS)).astype(BF16)
         dqkv[lo : lo + QB, 2 * HD :] = nn(pt[lo : lo + QB, lo:], rows(3, lo, SLOTS)).astype(BF16)
 
+    wait(rxp.at[:, core], x_recv)
+    remote(rxp.at[:, core], rxp.at[:, core], fx_send, fx_recv, (sib, m))
     mine = dqkv[pl.ds(pl.multiple_of(8 * PM * c + 4 * PM * core, 4 * PM), 4 * PM), :]
-    u = nt(mine, wcat[...]).astype(BF16)
+    u = nn(mine, wcat[...]).astype(BF16)
     for t in range(4):
         us[t] = u[t * PM : (t + 1) * PM]
     owner0 = 8 * c + 4 * core
 
     def send_u(far):
         for t in range(4):
-            remote(us.at[t], ru.at[NH * m + h], u_send, u_recv.at[m, h // 2], (owner0 + t, far))
+            remote(us.at[t], ru.at[NH * m + h], u_send, u_recv.at[m, h], (owner0 + t, far))
+
+    for t in range(4):
+
+        @pl.when(owner0 + t == me)
+        def _():
+            local(us.at[t], ru.at[NH * m + h], u_recv.at[m, h])
+
+        @pl.when(owner0 + t != me)
+        def _():
+            remote(us.at[t], ru.at[NH * m + h], u_send, u_recv.at[m, h], (owner0 + t, m))
 
     @pl.when(h < 2)
     def _():
@@ -223,45 +234,19 @@
         send_u(behind)
         send_u(ahead)
 
-    for t in range(4):
-
-        @pl.when(owner0 + t == me)
-        def _():
-            local(us.at[t], ru.at[NH * m + h], u_recv.at[m, h // 2])
-
-        @pl.when(owner0 + t != me)
-        def _():
-            remote(us.at[t], ru.at[NH * m + h], u_send, u_recv.at[m, h // 2], (owner0 + t, m))
-
-    wait(rxp.at[:, 1 - core], fx_recv)
-    gsend[...] = tn(rxp[...].reshape(SLOTS, HD), dqkv[...])
-    for t in range(4):
-        src = gsend.at[pl.ds(pl.multiple_of(4 * PM * core + t * PM, PM), PM)]
-
-        @pl.when(owner0 + t == me)
-        def _():
-            local(src, rg.at[h], g_recv)
-
-        @pl.when(owner0 + t != me)
-        def _():
-            remote(src, rg.at[h], g_send, g_recv, (owner0 + t, m))
-
     for dm in range(1, NM):
         wait(rp.at[0], pool_recv.at[dm - 1])
-    rp_all = rp[...].reshape(NM * PM, DB)
-    sc_all = nt(rp_all, x)
+    sc_all = nt(rp[...].reshape(NM * PM, DB), x)
     for i in range(NM * NH):
         row = (i // NH) * PM + i % NH
         a_all[i * PM : (i + 1) * PM] = pool_softmax(sc_all[row : row + 1], member)
 
-    def heads(group, first, n):
-        return pl.ds(NH * group + first, n)
-
-    def arrived(group, part):
-        wait(ru.at[pl.ds(0, 2)], u_recv.at[group, part])
+    def arrived(group, first, n):
+        for i in range(first, first + n):
+            wait(ru.at[0], u_recv.at[group, i])
 
     def group_of(group):
-        u_g = ru[heads(group, 0, NH)].reshape(NH * PM, DB)
+        u_g = ru[pl.ds(NH * group, NH)].reshape(NH * PM, DB)
         a_g = a_all[pl.ds(pl.multiple_of(NH * PM * group, NH * PM), NH * PM), :]
         ad = a_g * nt(u_g, x)
         d = ad - a_g * jnp.sum(ad, axis=1, keepdims=True)
@@ -270,8 +255,7 @@
         left = jnp.concatenate([a_g.astype(BF16), ds_g], axis=0)
         return ds_g, left, jnp.concatenate([u_g, rp[group]], axis=0)
 
-    arrived(m, 0)
-    arrived(m, 1)
+    arrived(m, 0, NH)
     ds_own, left, right = group_of(m)
     part = nn(ds_own, x)
     for i in range(NC):
@@ -286,10 +270,24 @@
     lax.fori_loop(1, NC, send_s, 0)
 
     opposite = lax.rem(m + 2, NM)
-    arrived(behind, 0)
-    remote(ru.at[heads(behind, 0, 2)], ru.at[heads(behind, 0, 2)], v_send.at[0], u_recv.at[behind, 0], (me, ahead))
-    arrived(ahead, 1)
-    remote(ru.at[heads(ahead, 2, 2)], ru.at[heads(ahead, 2, 2)], v_send.at[1], u_recv.at[ahead, 1], (me, behind))
+    for i in range(2):
+        for n, (group, to, head) in enumerate(((behind, ahead, i), (ahead, behind, 2 + i))):
+            arrived(group, head, 1)
+            block = ru.at[NH * group + head]
+            remote(block, block, v_send.at[n, i], u_recv.at[group, head], (me, to))
+
+    wait(rxp.at[:, 1 - core], fx_recv)
+    gsend[...] = tn(rxp[...].reshape(SLOTS, HD), dqkv[...])
+    for t in range(4):
+        src = gsend.at[pl.ds(pl.multiple_of(4 * PM * core + t * PM, PM), PM)]
+
+        @pl.when(owner0 + t == me)
+        def _():
+            local(src, rg.at[h], g_recv)
+
+        @pl.when(owner0 + t != me)
+        def _():
+            remote(src, rg.at[h], g_send, g_recv, (owner0 + t, m))
 
     acc[...] = tn(left, right)
 
@@ -303,10 +301,10 @@
 
     lax.fori_loop(1, 8, send_t, 0)
 
-    arrived(behind, 1)
+    arrived(behind, 2, 2)
     _, left, right = group_of(behind)
     acc[...] += tn(left, right)
-    arrived(ahead, 0)
+    arrived(ahead, 0, 2)
     _, left, right = group_of(ahead)
     acc[...] += tn(left, right)
 
@@ -321,8 +319,7 @@
     gs_v[...] = tot[:NH, :PM]
     out_s = local(gs_v, gs_hbm, out_sem.at[1])
 
-    arrived(opposite, 0)
-    arrived(opposite, 1)
+    arrived(opposite, 0, NH)
     _, left, right = group_of(opposite)
     out_x = []
     step = B // 4
@@ -337,8 +334,9 @@
     wait(rxp.at[pl.ds(0, NE - 1), 0], x_send)
     wait(rq.at[:, 0], f_send)
     wait(rxp.at[:, 0], fx_send)
-    wait(ru.at[pl.ds(0, 2)], v_send.at[0])
-    wait(ru.at[pl.ds(0, 2)], v_send.at[1])
+    for n in range(2):
+        for i in range(2):
+            wait(ru.at[0], v_send.at[n, i])
     own = half == core
 
     @pl.when(own)
@@ -394,7 +392,7 @@
         scratch_shapes=[
             pltpu.VMEM((B, DB), BF16),
             pltpu.VMEM((3, DB, NH * HD), BF16),
-            pltpu.VMEM((DB, 3 * HD), BF16),
+            pltpu.VMEM((3 * HD, DB), BF16),
             pltpu.VMEM((PM, DB), BF16),
             pltpu.VMEM((NH, PM, 4 * HD), BF16),
             pltpu.VMEM((NC, NH * PM, HD), BF16),
@@ -425,8 +423,8 @@
             dma, dma,
             dma, dma,
             dma, dma,
-            dma, dma((NM, 2)),
-            dma((2,)),
+            dma, dma((NM, NH)),
+            dma((2, 2)),
             dma, dma,
             dma, dma,
             dma, dma,

time: 46.5 us -> 44.8 us (0.963)
  Pallas kernels: 45.6 us -> 43.6 us
    pallas_call x1, Pallas kernels: 43.4 us -> 41.4 us  [shards(): pl.pallas_call(kernel, out_shape=(x_shape, jax.ShapeDtypeStruct((3, PM, N...]
where the time goes in v3:
time: 44.8 us; the launch traced here: 44.3 us
  Pallas kernels  43.6 us (97%)
  between operations  0.64 us (1%)
    pallas_call x1, Pallas kernels, shards(): pl.pallas_call(kernel, out_shape=(x_shape, jax.ShapeDtypeStruct((3, PM, N...  41.4 us
    pallas_call x1, Pallas kernels, shards(): pl.pallas_call(emit, out_shape=(x_shape, w_shape, w_shape, w_shape, s_sha...  2.18 us

profile of v3, /device:TPU:1, one launch (start us, length us, event | category | flops | bytes accessed | tf_op | source)
XLA Modules:
  0.0 44.3 jit_solution(10786209410539107491)
XLA Ops:
  0.6 41.4 %shard_map.110 = (bf16[512,1024]{1,0:T(8,128)(2,1)}, f32[3,16,512]{2,1,0:T(8,128)}, f32[4,16]{1,0:T(4,128)}) custom-call(bf16[512,1024]{1,0:T(8,128)(2,1)} %x_hbm.1, s32[1,512]{1,0:T(1,128)} %ids_ref.1, bf16[4,1024]{1,0:T(4,128)(2,1)} %bitcast.2, bf16[1024,512]{1,0:T(8,128)(2,1)} %wq_hbm.1, bf16[1024,512]{1,0:T(8,128)(2,1)} %wk_hbm.1, ...), custom_call_target="tpu_custom_call" | custom-call | tf_op jit(solution)/shard_map/pallas_call | solution.py:387
  42.1 2.2 %shard_map.111 = (bf16[512,1024]{1,0:T(8,128)(2,1)}, f32[16,512]{1,0:T(8,128)}, f32[16,512]{1,0:T(8,128)}, f32[16,512]{1,0:T(8,128)}, f32[4,16]{1,0:T(4,128)}) custom-call(bf16[512,1024]{1,0:T(8,128)(2,1)} %get-tuple-element.13.dx_in, f32[3,16,512]{2,1,0:T(8,128)} %get-tuple-element.14.gw_in, f32[4,16]{1,0:T(4,128)} %get-tuple-element.15.gs_in), custom_call_target="tpu_custom_call" | custom-call | tf_op jit(solution)/shard_map/pallas_call | solution.py:437

commit v4 on v3

--- a/solution.py
+++ b/solution.py
@@ -11,7 +11,7 @@
 NM = 4
 NS = 64
 NE = 32
-EMIT = 8
+EMIT = 4
 NC = 8
 B = 512
 DB = 1024
@@ -62,7 +62,7 @@
 def kernel(
     x_hbm, ids_ref, pool_ref, wq_hbm, wk_hbm, wv_hbm, g_ref,
     dx_hbm, gw_hbm, gs_hbm,
-    x_v, w_v, wcat, pool_v, qs, xps, rq, rxp, rp, kc, bias, pt, dst, dqkv, us, ru, gsend, rg, sc_send, rs, tot_send, rt, a_all, acc, dx_v, gw_v, gs_v,
+    x_v, w_v, wcat, pool_v, qs, xps, rq, rxp, rp, kc, bias, pt, dst, kt_v, dc, dqkv, us, ru, gsend, rg, sc_send, rs, tot_send, rt, a_all, acc, dx_v, gw_v, gs_v,
     in_sem, pool_send, pool_recv, q_send, q_recv, x_send, x_recv, f_send, f_recv, fx_send, fx_recv,
     u_send, u_recv, v_send, g_send, g_recv, s_send, s_recv, t_send, t_recv, out_sem,
 ):
@@ -150,6 +150,20 @@
         to = chip(off)
         remote(qs.at[to % 4], rq.at[e, core], q_send, q_recv, (2 * to + core, m))
 
+    rp[m] = pool_v[...]
+    for dm in range(1, NM):
+        remote(pool_v, rp.at[m], pool_send.at[dm - 1], pool_recv.at[dm - 1], (me, lax.rem(m + dm, NM)))
+
+    col = pl.ds(pl.multiple_of(h * HD, HD), HD)
+    for j in range(3):
+        wcat[j * HD : (j + 1) * HD, :] = w_v[j, :, col].T
+
+    for j in range(1, SLOTS // QB):
+        blank = jnp.zeros((QB, j * QB), BF16)
+        pt[j * QB : (j + 1) * QB, : j * QB] = blank
+        dst[j * QB : (j + 1) * QB, : j * QB] = blank
+    wait(rq.at[:, core], q_recv)
+    remote(rq.at[:, core], rq.at[:, core], f_send, f_recv, (sib, m))
     def send_x(i, _):
         to = lax.rem(e + i, NE)
         src = xps.at[to // 4, pl.ds(pl.multiple_of((to % 4) * PM, PM), PM)]
@@ -158,23 +172,13 @@
 
     lax.fori_loop(1, NE, send_x, 0)
 
-    rp[m] = pool_v[...]
-    for dm in range(1, NM):
-        remote(pool_v, rp.at[m], pool_send.at[dm - 1], pool_recv.at[dm - 1], (me, lax.rem(m + dm, NM)))
-
-    col = pl.ds(pl.multiple_of(h * HD, HD), HD)
-    for j in range(3):
-        wcat[j * HD : (j + 1) * HD, :] = w_v[j, :, col].T
-
-    wait(rq.at[:, core], q_recv)
-    remote(rq.at[:, core], rq.at[:, core], f_send, f_recv, (sib, m))
     wait(rq.at[:, 1 - core], f_recv)
 
     k_raw = rq[:, :, :, HD : 2 * HD].reshape(SLOTS, HD).astype(F32)
     bad = k_raw > 0.5 * MARK
     kc[...] = jnp.where(bad, 0.0, k_raw).astype(BF16)
     bias[...] = jnp.where(bad, NEG, 0.0)
-    k_t = kc[...].T
+    kt_v[...] = kc[...].T
 
     def rows(lane, lo, hi):
         return rq[lo // 32 : hi // 32, :, :, lane * HD : (lane + 1) * HD].reshape(hi - lo, HD)
@@ -196,15 +200,11 @@
         delta = jnp.sum(pb.astype(F32) * dp, axis=0, keepdims=True)
         ds = (p * (dp - delta) * SCALE).astype(BF16)
         dst[:n, lo:n] = ds
-        dqkv[lo:n, :HD] = nn(k_t[:, :n], ds).T.astype(BF16)
-    for j in range(SLOTS // QB):
-        lo = j * QB
-        dqkv[lo : lo + QB, HD : 2 * HD] = nn(dst[lo : lo + QB, lo:], rows(0, lo, SLOTS)).astype(BF16)
-        dqkv[lo : lo + QB, 2 * HD :] = nn(pt[lo : lo + QB, lo:], rows(3, lo, SLOTS)).astype(BF16)
-
-    wait(rxp.at[:, core], x_recv)
-    remote(rxp.at[:, core], rxp.at[:, core], fx_send, fx_recv, (sib, m))
-    mine = dqkv[pl.ds(pl.multiple_of(8 * PM * c + 4 * PM * core, 4 * PM), 4 * PM), :]
+    block = pl.ds(pl.multiple_of(HD * c, HD), HD)
+    dc[:, :HD] = nn(kt_v[...], dst[:, block]).T.astype(BF16)
+    dc[:, HD : 2 * HD] = nn(dst[block, :], rows(0, 0, SLOTS)).astype(BF16)
+    dc[:, 2 * HD :] = nn(pt[block, :], rows(3, 0, SLOTS)).astype(BF16)
+    mine = dc[pl.ds(pl.multiple_of(4 * PM * core, 4 * PM), 4 * PM), :]
     u = nn(mine, wcat[...]).astype(BF16)
     for t in range(4):
         us[t] = u[t * PM : (t + 1) * PM]
@@ -234,6 +234,8 @@
         send_u(behind)
         send_u(ahead)
 
+    wait(rxp.at[:, core], x_recv)
+    remote(rxp.at[:, core], rxp.at[:, core], fx_send, fx_recv, (sib, m))
     for dm in range(1, NM):
         wait(rp.at[0], pool_recv.at[dm - 1])
     sc_all = nt(rp[...].reshape(NM * PM, DB), x)
@@ -275,6 +277,14 @@
             arrived(group, head, 1)
             block = ru.at[NH * group + head]
             remote(block, block, v_send.at[n, i], u_recv.at[group, head], (me, to))
+
+    for i in range(SLOTS // QB):
+        lo, n = i * QB, (i + 1) * QB
+        dqkv[lo:n, :HD] = nn(kt_v[:, :n], dst[:n, lo:n]).T.astype(BF16)
+    for j in range(SLOTS // QB):
+        lo = j * QB
+        dqkv[lo : lo + QB, HD : 2 * HD] = nn(dst[lo : lo + QB, lo:], rows(0, lo, SLOTS)).astype(BF16)
+        dqkv[lo : lo + QB, 2 * HD :] = nn(pt[lo : lo + QB, lo:], rows(3, lo, SLOTS)).astype(BF16)
 
     wait(rxp.at[:, 1 - core], fx_recv)
     gsend[...] = tn(rxp[...].reshape(SLOTS, HD), dqkv[...])
@@ -403,6 +413,8 @@
             pltpu.VMEM((SLOTS, HD), F32),
             pltpu.VMEM((SLOTS, SLOTS), BF16),
             pltpu.VMEM((SLOTS, SLOTS), BF16),
+            pltpu.VMEM((HD, SLOTS), BF16),
+            pltpu.VMEM((HD, 3 * HD), BF16),
             pltpu.VMEM((SLOTS, 3 * HD), BF16),
             pltpu.VMEM((4, PM, DB), BF16),
             pltpu.VMEM((NM * NH, PM, DB), BF16),

time: 44.8 us -> 44.2 us (0.987)
  no operation moved by 1% of the time
where the time goes in v4:
time: 44.2 us; the launch traced here: 44 us
  Pallas kernels  43.4 us (98%)
  between operations  0.64 us (1%)
    pallas_call x1, Pallas kernels, shards(): pl.pallas_call(kernel, out_shape=(x_shape, jax.ShapeDtypeStruct((3, PM, N...  41.3 us
    pallas_call x1, Pallas kernels, shards(): pl.pallas_call(emit, out_shape=(x_shape, w_shape, w_shape, w_shape, s_sha...  2.07 us

profile of v4, /device:TPU:1, one launch (start us, length us, event | category | flops | bytes accessed | tf_op | source)
XLA Modules:
  0.0 44.0 jit_solution(6801445300678578144)
XLA Ops:
  0.6 41.3 %shard_map.110 = (bf16[512,1024]{1,0:T(8,128)(2,1)}, f32[3,16,512]{2,1,0:T(8,128)}, f32[4,16]{1,0:T(4,128)}) custom-call(bf16[512,1024]{1,0:T(8,128)(2,1)} %x_hbm.1, s32[1,512]{1,0:T(1,128)} %ids_ref.1, bf16[4,1024]{1,0:T(4,128)(2,1)} %bitcast.2, bf16[1024,512]{1,0:T(8,128)(2,1)} %wq_hbm.1, bf16[1024,512]{1,0:T(8,128)(2,1)} %wk_hbm.1, ...), custom_call_target="tpu_custom_call" | custom-call | tf_op jit(solution)/shard_map/pallas_call | solution.py:397
  41.9 2.1 %shard_map.111 = (bf16[512,1024]{1,0:T(8,128)(2,1)}, f32[16,512]{1,0:T(8,128)}, f32[16,512]{1,0:T(8,128)}, f32[16,512]{1,0:T(8,128)}, f32[4,16]{1,0:T(4,128)}) custom-call(bf16[512,1024]{1,0:T(8,128)(2,1)} %get-tuple-element.13.dx_in, f32[3,16,512]{2,1,0:T(8,128)} %get-tuple-element.14.gw_in, f32[4,16]{1,0:T(4,128)} %get-tuple-element.15.gs_in), custom_call_target="tpu_custom_call" | custom-call | tf_op jit(solution)/shard_map/pallas_call | solution.py:449

commit v5 on v4

--- a/solution.py
+++ b/solution.py
@@ -164,14 +164,6 @@
         dst[j * QB : (j + 1) * QB, : j * QB] = blank
     wait(rq.at[:, core], q_recv)
     remote(rq.at[:, core], rq.at[:, core], f_send, f_recv, (sib, m))
-    def send_x(i, _):
-        to = lax.rem(e + i, NE)
-        src = xps.at[to // 4, pl.ds(pl.multiple_of((to % 4) * PM, PM), PM)]
-        remote(src, rxp.at[e, core], x_send, x_recv, (2 * to + core, m))
-        return 0
-
-    lax.fori_loop(1, NE, send_x, 0)
-
     wait(rq.at[:, 1 - core], f_recv)
 
     k_raw = rq[:, :, :, HD : 2 * HD].reshape(SLOTS, HD).astype(F32)
@@ -234,8 +226,14 @@
         send_u(behind)
         send_u(ahead)
 
-    wait(rxp.at[:, core], x_recv)
-    remote(rxp.at[:, core], rxp.at[:, core], fx_send, fx_recv, (sib, m))
+    def send_x(i, _):
+        to = lax.rem(e + i, NE)
+        src = xps.at[to // 4, pl.ds(pl.multiple_of((to % 4) * PM, PM), PM)]
+        remote(src, rxp.at[e, core], x_send, x_recv, (2 * to + core, m))
+        return 0
+
+    lax.fori_loop(1, NE, send_x, 0)
+
     for dm in range(1, NM):
         wait(rp.at[0], pool_recv.at[dm - 1])
     sc_all = nt(rp[...].reshape(NM * PM, DB), x)
@@ -278,6 +276,8 @@
             block = ru.at[NH * group + head]
             remote(block, block, v_send.at[n, i], u_recv.at[group, head], (me, to))
 
+    wait(rxp.at[:, core], x_recv)
+    remote(rxp.at[:, core], rxp.at[:, core], fx_send, fx_recv, (sib, m))
     for i in range(SLOTS // QB):
         lo, n = i * QB, (i + 1) * QB
         dqkv[lo:n, :HD] = nn(kt_v[:, :n], dst[:n, lo:n]).T.astype(BF16)

time: 44.2 us -> 47.3 us (1.070)
  Pallas kernels: 43.4 us -> 46.4 us
    pallas_call x1, Pallas kernels: 41.3 us -> 44.3 us  [shards(): pl.pallas_call(kernel, out_shape=(x_shape, jax.ShapeDtypeStruct((3, PM, N...]
where the time goes in v5:
time: 47.3 us; the launch traced here: 47.1 us
  Pallas kernels  46.4 us (98%)
  between operations  0.64 us (1%)
    pallas_call x1, Pallas kernels, shards(): pl.pallas_call(kernel, out_shape=(x_shape, jax.ShapeDtypeStruct((3, PM, N...  44.3 us
    pallas_call x1, Pallas kernels, shards(): pl.pallas_call(emit, out_shape=(x_shape, w_shape, w_shape, w_shape, s_sha...  2.07 us

profile of v5, /device:TPU:1, one launch (start us, length us, event | category | flops | bytes accessed | tf_op | source)
XLA Modules:
  0.0 47.1 jit_solution(14405671720967973445)
XLA Ops:
  0.6 44.3 %shard_map.110 = (bf16[512,1024]{1,0:T(8,128)(2,1)}, f32[3,16,512]{2,1,0:T(8,128)}, f32[4,16]{1,0:T(4,128)}) custom-call(bf16[512,1024]{1,0:T(8,128)(2,1)} %x_hbm.1, s32[1,512]{1,0:T(1,128)} %ids_ref.1, bf16[4,1024]{1,0:T(4,128)(2,1)} %bitcast.2, bf16[1024,512]{1,0:T(8,128)(2,1)} %wq_hbm.1, bf16[1024,512]{1,0:T(8,128)(2,1)} %wk_hbm.1, ...), custom_call_target="tpu_custom_call" | custom-call | tf_op jit(solution)/shard_map/pallas_call | solution.py:397
  45.0 2.1 %shard_map.111 = (bf16[512,1024]{1,0:T(8,128)(2,1)}, f32[16,512]{1,0:T(8,128)}, f32[16,512]{1,0:T(8,128)}, f32[16,512]{1,0:T(8,128)}, f32[4,16]{1,0:T(4,128)}) custom-call(bf16[512,1024]{1,0:T(8,128)(2,1)} %get-tuple-element.13.dx_in, f32[3,16,512]{2,1,0:T(8,128)} %get-tuple-element.14.gw_in, f32[4,16]{1,0:T(4,128)} %get-tuple-element.15.gs_in), custom_call_target="tpu_custom_call" | custom-call | tf_op jit(solution)/shard_map/pallas_call | solution.py:449
